TPU v7x, 512 devices: a whole 4x8x8 slice. The times are simulated.
512 devices in a mesh: rows: 32 (over y, x_hi, core), ctr: 16 (over z, x_lo).
Axes of the slice: x: 4 (x_hi: 2, x_lo: 2; x = x_hi * 2 + x_lo), y: 8, z: 8, core: 2. Of those that a mesh axis runs over, the one named last changes fastest.
Arguments:
- points: bfloat16 [32768, 1024], P('rows'), may hold values from -24 to 24
- centers: bfloat16 [8192, 1024], P('ctr'), may hold values from -6 to 6
- assignment: int32 [32768], P('rows'), may hold values from 0 to 8191, as said below
- row_weight: float32 [32768], P('rows'), may hold values from 0.25 to 4
Outputs:
- row_share: float32 [32768], P(('rows', 'ctr'))
- centroid: float32 [8192, 1024], P(('ctr', 'rows'))
- cluster_share: float32 [8192], P(('ctr', 'rows'))
Inputs may be any that keep to these rules, and one draw needn't show every extreme that they name: Row i belongs to cluster assignment[i]. In each aligned block of 1024 rows, at most 4 rows name clusters of any one aligned run of 16 clusters (r * 16 to r * 16 + 15); one such run holds exactly 4 rows of every block.
All inputs are finite; a program needn't handle non-finite values.
Results may differ from a plain program's by a relative error of at most 0.0025.
Values may be sent and summed in bfloat16 or wider, within the bound.
A program may use at most 64 MiB of HBM per device.

v0:
```python
import jax
import jax.numpy as jnp
from jax import lax
from jax.sharding import PartitionSpec as P


def local(points, centers, assignment, row_weight):
    slab_rows = points.shape[0]
    block_size = centers.shape[0]
    rows_size = lax.axis_size("rows")
    ctr_size = lax.axis_size("ctr")
    run_size = block_size // rows_size
    own_size = slab_rows // ctr_size
    ctr_index = lax.axis_index("ctr")
    point_norm = jnp.sum(jnp.square(points.astype(jnp.float32)), axis=1)
    center_norm = jnp.sum(jnp.square(centers.astype(jnp.float32)), axis=1)
    cross_term = jnp.dot(points, centers.T, preferred_element_type=jnp.float32)
    partial_min = jnp.min(point_norm[:, None] - 2.0 * cross_term + center_norm[None, :], axis=1)
    local_id = assignment - ctr_index * block_size
    weighted_points = (points.astype(jnp.float32) * row_weight[:, None]).astype(jnp.bfloat16)
    labels = lax.broadcasted_iota(jnp.int32, (1, lax.axis_size("rows") * run_size), 1)
    member = (local_id[:, None] == labels).astype(jnp.bfloat16)
    coord_sums = lax.psum_scatter(
        lax.dot_general(
            member, weighted_points, (((0,), (0,)), ((), ())), preferred_element_type=jnp.float32
        ),
        "rows",
        scatter_dimension=0,
        tiled=True,
    )
    nearest = lax.pmin(partial_min, "ctr")
    weighted_cost = nearest * row_weight
    block_hot = (local_id[:, None] == lax.broadcasted_iota(jnp.int32, (1, block_size), 1)).astype(
        jnp.float32
    )
    cost_local = jnp.dot(weighted_cost, block_hot, precision=lax.Precision.HIGHEST)
    count_local = jnp.dot(row_weight, block_hot, precision=lax.Precision.HIGHEST)
    own_near = lax.dynamic_slice_in_dim(nearest, ctr_index * own_size, own_size)
    cost_own, count_own = (
        lax.psum_scatter(cost_local, "rows", scatter_dimension=0, tiled=True),
        lax.psum_scatter(count_local, "rows", scatter_dimension=0, tiled=True),
    )
    cost_all, count_all = (
        lax.all_gather(cost_own, ("rows", "ctr"), axis=0, tiled=True),
        lax.all_gather(count_own, ("rows", "ctr"), axis=0, tiled=True),
    )
    total_cost, total_weight = lax.psum((jnp.sum(weighted_cost), jnp.sum(row_weight)), "rows")
    own_ids = lax.dynamic_slice_in_dim(assignment, ctr_index * own_size, own_size)
    holder = own_ids // block_size
    within = own_ids % block_size
    slot_index = within // run_size * (ctr_size * run_size) + holder * run_size + within % run_size
    cost_row = jnp.take(cost_all, slot_index)
    count_row = jnp.take(count_all, slot_index)
    mean_cost = total_cost / total_weight
    size_own = jnp.maximum(count_own, 1.0)
    centroid = coord_sums / size_own[:, None]
    cluster_share = cost_own / (size_own * mean_cost)
    row_share = own_near / mean_cost + 2.0 * (cost_row / (jnp.maximum(count_row, 1.0) * mean_cost))
    return (row_share, centroid, cluster_share)


def solution(mesh):
    placed = (P("rows", None), P("ctr", None), P("rows"), P("rows"))
    return jax.shard_map(
        local,
        mesh=mesh,
        in_specs=placed,
        out_specs=(P(("rows", "ctr")), P(("ctr", "rows"), None), P(("ctr", "rows"))),
        check_vma=False,
    )
```

profile of v0, /device:TPU:1, one launch (start us, length us, event | category | flops | bytes accessed | tf_op | source)
XLA Modules:
  0.0 395.1 jit_solution(12898436087304975150)
XLA Ops:
  8.0 0.0 all-reduce.8.cloned.1.call-start
  8.1 1.7 multiply_reduce_fusion
  9.7 2.1 fusion
  11.8 0.0 copy-start.4
  11.8 1.3 add_reduce_fusion
  13.2 34.4 %pmin.7 = f32[1024]{0:T(1024)S(1)} all-reduce(f32[1024]{0:T(1024)S(1)} %add_reduce_fusion), channel_id=1, replica_groups=mesh['rows'=32,'ctr'=16] {'ctr'}, use_global_device_ids=true, to_apply=%region_3.0 | all-reduce | flops 1024 | bytes 8192 | tf_op jit(solution)/shard_map/pmin | solution.py:31
  47.6 0.6 fusion.13
  48.2 0.8 fusion.5
  49.0 0.8 fusion.6
  49.8 1.3 dynamic-slice
  51.7 74.1 %all-reduce.5 = (f32[512]{0:T(512)S(1)}, f32[512]{0:T(512)S(1)}, f32[]{:T(128)}, f32[]{:T(128)}) all-reduce(f32[512]{0:T(512)S(1)} %bitcast.11, f32[512]{0:T(512)S(1)} %bitcast.12, f32[]{:T(128)} %get-tuple-element.10, f32[]{:T(128)} %get-tuple-element.12), channel_id=3, replica_groups=mesh['rows'=32,'ctr'=16] {'rows'}, use_global_device_ids=true, to_apply=%region_9.11.clone | all-reduce | flops 1026 | bytes 8208
  127.1 0.2 dynamic-slice_dynamic-update-slice_fusion.1
  127.3 0.6 multiply_divide_fusion
  128.0 0.6 copy-done.2
  128.6 0.0 all-reduce.8.cloned.1.call-update
  128.6 0.0 reduce-scatter.2.cloned.1.call-start
  128.7 2.8 fusion.2
  131.5 0.0 reduce-scatter.2.cloned.1.call-update
  131.5 0.1 compare_select_fusion
  131.6 250.9 %all-reduce.8.cloned.1.call-done = (f32[8192]{0:T(1024)}, f32[8192]{0:T(1024)}) async-done(((f32[8192]{0:T(1024)}, f32[8192]{0:T(1024)}), (f32[8192]{0:T(1024)}, f32[8192]{0:T(1024)})) %all-reduce.8.cloned.1.call-update) | async-done | bytes 65552
  382.5 1.5 gather_fusion.1
  384.0 1.5 gather_fusion
  385.5 0.6 divide_add_fusion
  386.1 1.5 broadcast_divide_fusion
  (15 shorter events, 0.0 us)
Async XLA Ops:
  8.0 3.8 copy-start.1
  8.0 3.8 copy-start
  8.0 374.4 %all-reduce.8.cloned.1.call-start = ((), (), s32[]{:S(2)}) async-start(), calls=%async_computation.2 | async-start | bytes 131072
  11.8 35.7 %copy-start.4 = (s32[1024]{0:T(1024)S(1)}, s32[1024]{0:T(1024)}, u32[]{:S(2)}) copy-start(s32[1024]{0:T(1024)} %param.8) | copy-start | bytes 12292
  11.8 35.7 %copy-start.5 = (f32[1024]{0:T(1024)S(1)}, f32[1024]{0:T(1024)}, u32[]{:S(2)}) copy-start(f32[1024]{0:T(1024)} %param.9) | copy-start | bytes 12292
  127.3 0.6 copy-start.3
  128.0 0.6 copy-start.2
  128.6 257.5 %reduce-scatter.2.cloned.1.call-start = ((), (), s32[]{:S(2)}) async-start(), calls=%async_computation.1 | async-start | bytes 2162688 | tf_op jit(solution)/shard_map/reduce_scatter | solution.py:23
Sparse Core Ops, SparseCore 0:
  128.7 253.6 all-reduce.7
Sparse Core Ops, SparseCore 1:
  134.5 115.6 reduce-scatter.1
where the time goes:
time: 396 us; the launch traced here: 395 us
  waiting for transfers between devices  251 us (63%)
  blocking collectives  108 us (27%)
  between operations  17.6 us (4%)
  other arithmetic  7.24 us (2%)
  matrix products  5.72 us (1%)
  local copies, waits for them, and re-layouts  5.18 us (1%)
    unnamed x3, waiting for transfers between devices  251 us
    unnamed x1, blocking collectives  74.1 us
    pmin x1, blocking collectives, local(): nearest = lax.pmin(partial_min, 'ctr')  34.4 us
  transfers between devices with their start and end apart: 2, of which 1 were waited for; matrix products, arithmetic and copies ran while one was open for 2% of the time, Pallas kernels for 0%

commit v1 on v0

v1 whole, which is shorter than its diff:
```python
import functools

import jax
import jax.numpy as jnp
from jax import lax
from jax.experimental import pallas as pl
from jax.experimental.pallas import tpu as pltpu
from jax.sharding import PartitionSpec as P

KO = 16
CAP = 4
LANES = 128
MESH = pl.DeviceIdType.MESH
F32 = jnp.float32
BF16 = jnp.bfloat16


def iota(shape, dim):
    return lax.broadcasted_iota(jnp.int32, shape, dim)


def dot_nt(a, b):
    return lax.dot_general(a, b, (((1,), (1,)), ((), ())), preferred_element_type=F32)


def dot_nn(a, b):
    return lax.dot_general(a, b, (((1,), (0,)), ((), ())), preferred_element_type=F32)


def split3(x):
    hi = x.astype(BF16).astype(F32)
    mid = (x - hi).astype(BF16).astype(F32)
    lo = ((x - hi) - mid).astype(BF16).astype(F32)
    return [hi, mid, lo]


def spread(parts):
    stack = jnp.concatenate(parts, axis=0)
    block = iota(stack.shape, 0) & 7
    return jnp.concatenate([jnp.where(block == b, stack, 0.0) for b in range(8)], axis=1).astype(BF16)


def group_sum(x):
    lane = iota(x.shape, 1)
    x = x + jnp.where(lane & 1 == 0, pltpu.roll(x, LANES - 1, 1), pltpu.roll(x, 1, 1))
    return x + jnp.where(lane & 2 == 0, pltpu.roll(x, LANES - 2, 1), pltpu.roll(x, 2, 1))


def kernel(
    n_rows,
    n_ctr,
    points_hbm,
    centers_hbm,
    assign_ref,
    weight_ref,
    row_share_ref,
    centroid_ref,
    share_ref,
    points,
    centers,
    pick,
    rows_out,
    rows_in,
    min_out,
    min_in,
    slot_out,
    slot_in,
    back_out,
    back_in,
    near_ref,
    ids_ref,
    load_sem,
    rows_sems,
    min_sems,
    slot_sems,
    back_sems,
):
    s = lax.axis_index("rows")
    c = lax.axis_index("ctr")
    chunk = points.shape[0] // 4

    center_load = pltpu.make_async_copy(centers_hbm, centers, load_sem.at[4])
    center_load.start()
    point_loads = []
    for q in range(4):
        part = pl.ds(q * chunk, chunk)
        load = pltpu.make_async_copy(points_hbm.at[part], points.at[part], load_sem.at[q])
        load.start()
        point_loads.append(load)

    def row_peers(act):
        def step(d, carry):
            act(lax.rem(s + d, n_rows))
            return carry

        lax.fori_loop(1, n_rows, step, 0)

    def ctr_peers(act):
        def step(d, carry):
            act(lax.rem(c + d, n_ctr))
            return carry

        lax.fori_loop(1, n_ctr, step, 0)

    barrier = pltpu.get_barrier_semaphore()
    row_peers(lambda r: pl.semaphore_signal(barrier, inc=1, device_id=(r, c), device_id_type=MESH))
    ctr_peers(lambda p: pl.semaphore_signal(barrier, inc=1, device_id=(s, p), device_id_type=MESH))

    assign = assign_ref[...]
    weight = weight_ref[...]
    run = (assign >> 4) - c * n_rows
    member = (assign & (KO - 1)).astype(F32)
    hot = [(run[b : b + 1, :] == iota((n_rows, LANES), 0)).astype(F32) for b in range(8)]
    before = jnp.concatenate(
        [
            (iota((LANES, LANES), 0) < iota((LANES, LANES), 1)).astype(F32),
            jnp.ones((LANES, LANES), F32),
        ],
        axis=1,
    ).astype(BF16)
    counted = dot_nn(jnp.concatenate(hot, axis=0).astype(BF16), before)
    carry = jnp.zeros((n_rows, LANES), F32)
    for b in range(8):
        rank = counted[b * n_rows : (b + 1) * n_rows, :LANES] + carry
        carry = carry + counted[b * n_rows : (b + 1) * n_rows, LANES:]
        rank = jnp.sum(hot[b] * rank, axis=0, keepdims=True).astype(jnp.int32)
        here = run[b : b + 1, :]
        code = jnp.where((here >= 0) & (here < n_rows), here * CAP + rank, -1)
        lanes = pl.ds(b * LANES, LANES)
        pick[0:LANES, lanes] = (iota((LANES, LANES), 0) == code).astype(F32).astype(BF16)
        at = iota((2 * LANES, LANES), 0)
        at = (at >> 3) * CAP + (at & (CAP - 1))
        pick[LANES : 3 * LANES, lanes] = (at == code).astype(F32).astype(BF16)

    traits = spread([member + 1.0] + split3(weight))
    picked = dot_nt(traits, pick[0:LANES, :])
    slot_id = jnp.sum(picked[0:8], axis=0, keepdims=True) - 1.0
    slot_weight = jnp.sum(picked[8:32], axis=0, keepdims=True)
    slot_out[:, 0:LANES] = slot_id
    slot_out[:, LANES : 2 * LANES] = slot_weight
    slot_out[:, 2 * LANES : 3 * LANES] = jnp.sum(weight, axis=0, keepdims=True)

    row_weight = jnp.sum(dot_nt(pick[LANES : 3 * LANES, :], traits[8:32]), axis=1, keepdims=True)
    for load in point_loads:
        load.wait()
    half = (iota((2 * LANES, 256), 0) >> 2) & 1
    tiles = []
    for t in range(2):
        low = dot_nn(pick[LANES : 3 * LANES, :], points[:, pl.ds(2 * t * 256, 256)])
        high = dot_nn(pick[LANES : 3 * LANES, :], points[:, pl.ds((2 * t + 1) * 256, 256)])
        tiles.append((jnp.where(half == 0, low, high) * row_weight).reshape(n_rows, 8, 256))
    rows_out[...] = jnp.concatenate(tiles, axis=1).astype(BF16)

    center_load.wait()
    wide = centers[...].astype(F32)
    half_norm = 0.5 * jnp.sum(wide * wide, axis=1, keepdims=True)
    norms = []
    for q in range(4):
        some = points[q * chunk : (q + 1) * chunk, :]
        wide = some.astype(F32)
        wide = wide * wide
        total = wide[:, 0:LANES]
        for k in range(1, 8):
            total = total + wide[:, k * LANES : (k + 1) * LANES]
        norm = jnp.sum(total.T, axis=0, keepdims=True)
        least = jnp.min(half_norm - dot_nt(centers[...], some), axis=0, keepdims=True)
        for k in range(2):
            min_out[2 * q + k : 2 * q + k + 1, :] = least[:, k * LANES : (k + 1) * LANES]
            near_ref[2 * q + k : 2 * q + k + 1, :] = norm[:, k * LANES : (k + 1) * LANES]

    pl.semaphore_wait(barrier, n_rows + n_ctr - 2)

    def send_min(p):
        return pltpu.make_async_remote_copy(
            min_out, min_in.at[c], min_sems.at[0], min_sems.at[1], device_id=(s, p), device_id_type=MESH
        )

    def send_rows(r):
        return pltpu.make_async_remote_copy(
            rows_out.at[r], rows_in.at[s], rows_sems.at[0], rows_sems.at[1], device_id=(r, c), device_id_type=MESH
        )

    def send_slot(r):
        return pltpu.make_async_remote_copy(
            slot_out, slot_in.at[s], slot_sems.at[0], slot_sems.at[1], device_id=(r, c), device_id_type=MESH
        )

    def send_back(p):
        return pltpu.make_async_remote_copy(
            back_out.at[p // 2], back_in.at[c], back_sems.at[0], back_sems.at[1], device_id=(s, p), device_id_type=MESH
        )

    def wait_all(ref, count, sem):
        whole = ref.at[pl.ds(0, count)]
        pltpu.make_async_copy(whole, whole, sem).wait()

    ctr_peers(lambda p: send_min(p).start())
    row_peers(lambda r: send_rows(r).start())
    min_in[c] = min_out[...]
    rows_in[s] = rows_out[s]

    wait_all(min_in, n_ctr - 1, min_sems.at[1])
    near = near_ref[...] + 2.0 * jnp.min(min_in[...], axis=0)
    near_ref[...] = near
    cost = near * weight
    picked = dot_nt(spread(split3(cost)), pick[0:LANES, :])
    slot_out[:, 3 * LANES : 4 * LANES] = jnp.sum(picked, axis=0, keepdims=True)
    slot_out[:, 4 * LANES : 5 * LANES] = jnp.sum(cost, axis=0, keepdims=True)
    row_peers(lambda r: send_slot(r).start())
    slot_in[s] = slot_out[...]

    wait_all(slot_in, n_rows - 1, slot_sems.at[1])
    labels = iota((KO, LANES), 0).astype(F32)
    counts = jnp.zeros((KO, LANES), F32)
    costs = jnp.zeros((KO, LANES), F32)
    sums = jnp.zeros((1, LANES), F32)
    weights = jnp.zeros((1, LANES), F32)
    for r in range(n_rows):
        ids = slot_in[r, :, 0:LANES]
        mine = ids == labels
        counts = counts + jnp.where(mine, slot_in[r, :, LANES : 2 * LANES], 0.0)
        costs = costs + jnp.where(mine, slot_in[r, :, 3 * LANES : 4 * LANES], 0.0)
        weights = weights + slot_in[r, :, 2 * LANES : 3 * LANES]
        sums = sums + slot_in[r, :, 4 * LANES : 5 * LANES]
        ids_ref[r : r + 1, :] = ids
    mean = jnp.sum(sums, axis=1, keepdims=True) / jnp.sum(weights, axis=1, keepdims=True)
    size = jnp.maximum(group_sum(counts), 1.0)
    share = group_sum(costs) / (size * mean)
    slot_share = jnp.sum(jnp.where(slot_id == labels, share, 0.0), axis=0, keepdims=True)
    parts = jnp.concatenate(split3(slot_share) + [jnp.zeros((5, LANES), F32)], axis=0).astype(BF16)
    back = jnp.sum(dot_nn(parts, pick[0:LANES, :]), axis=0, keepdims=True)
    for b in range(8):
        back_out[b] = back[:, b * LANES : (b + 1) * LANES]
    ctr_peers(lambda p: send_back(p).start())
    back_in[c] = back_out[c // 2]

    own = iota((KO, LANES), 1) == s * CAP
    own_size = jnp.sum(jnp.where(own, size, 0.0), axis=1, keepdims=True)
    own_share = jnp.sum(jnp.where(own, share, 0.0), axis=1, keepdims=True)
    square = iota((KO, LANES), 0) == iota((KO, LANES), 1)
    share_ref[...] = jnp.sum(jnp.where(square, own_share, 0.0), axis=0, keepdims=True)[:, :KO]
    lane = iota((LANES, n_rows * KO), 1)
    at = iota((LANES, n_rows * KO), 0)
    place = (at == s * CAP + (lane & (CAP - 1))).astype(F32).astype(BF16)
    ids = dot_nn(ids_ref[...].astype(BF16), place)
    slab = iota((n_rows, n_rows * KO), 0) == iota((n_rows, n_rows * KO), 1) // KO
    ids = jnp.sum(jnp.where(slab, ids, 0.0), axis=0, keepdims=True).astype(jnp.int32)
    at = iota((4 * KO, n_rows * KO), 0)
    quarter = (iota((4 * KO, n_rows * KO), 1) & (KO - 1)) >> 2
    member = ((at & (KO - 1)) == ids) & ((at >> 4) == quarter)
    member = member.astype(F32).astype(BF16)
    wait_all(rows_in, n_rows - 1, rows_sems.at[1])
    coord = dot_nn(member, rows_in[...].reshape(n_rows * KO, 256))
    for q in range(4):
        centroid_ref[:, q * 256 : (q + 1) * 256] = coord[q * KO : (q + 1) * KO, :] / own_size

    wait_all(back_in, n_ctr - 1, back_sems.at[1])
    total = jnp.sum(back_in[...], axis=0)
    total = near_ref[pl.ds(c // 2, 1), :] / mean + 2.0 * total
    width = row_share_ref.shape[1]
    row_share_ref[...] = jnp.where(c % 2 == 0, total[:, :width], total[:, width : 2 * width])

    wait_all(min_in, n_ctr - 1, min_sems.at[0])
    wait_all(rows_in, n_rows - 1, rows_sems.at[0])
    wait_all(slot_in, n_rows - 1, slot_sems.at[0])
    wait_all(back_in, n_ctr - 1, back_sems.at[0])


def local(points, centers, assignment, row_weight):
    slab_rows, width = points.shape
    block = centers.shape[0]
    n_rows = lax.axis_size("rows")
    n_ctr = lax.axis_size("ctr")
    vmem = pl.BlockSpec(memory_space=pltpu.VMEM)
    hbm = pl.BlockSpec(memory_space=pl.ANY)
    row_share, centroid, share = pl.pallas_call(
        functools.partial(kernel, n_rows, n_ctr),
        out_shape=(
            jax.ShapeDtypeStruct((1, slab_rows // n_ctr), F32),
            jax.ShapeDtypeStruct((KO, width), F32),
            jax.ShapeDtypeStruct((1, KO), F32),
        ),
        in_specs=[hbm, hbm, vmem, vmem],
        out_specs=(vmem, vmem, vmem),
        scratch_shapes=[
            pltpu.VMEM((slab_rows, width), BF16),
            pltpu.VMEM((block, width), BF16),
            pltpu.VMEM((3 * LANES, slab_rows), BF16),
            pltpu.VMEM((n_rows, 16, 256), BF16),
            pltpu.VMEM((n_rows, 16, 256), BF16),
            pltpu.VMEM((8, LANES), F32),
            pltpu.VMEM((n_ctr, 8, LANES), F32),
            pltpu.VMEM((1, 5 * LANES), F32),
            pltpu.VMEM((n_rows, 1, 5 * LANES), F32),
            pltpu.VMEM((8, 1, LANES), F32),
            pltpu.VMEM((n_ctr, 1, LANES), F32),
            pltpu.VMEM((8, LANES), F32),
            pltpu.VMEM((n_rows, LANES), F32),
            pltpu.SemaphoreType.DMA((5,)),
            pltpu.SemaphoreType.DMA((2,)),
            pltpu.SemaphoreType.DMA((2,)),
            pltpu.SemaphoreType.DMA((2,)),
            pltpu.SemaphoreType.DMA((2,)),
        ],
        compiler_params=pltpu.CompilerParams(
            collective_id=0, has_side_effects=True, vmem_limit_bytes=48 * 1024 * 1024
        ),
        cost_estimate=pl.CostEstimate(
            flops=2 * slab_rows * width * (block + 3 * LANES),
            bytes_accessed=2 * (slab_rows + block) * width,
            transcendentals=0,
        ),
    )(points, centers, assignment.reshape(8, LANES), row_weight.reshape(8, LANES))
    return row_share.reshape(-1), centroid, share.reshape(-1)


def solution(mesh):
    placed = (P("rows", None), P("ctr", None), P("rows"), P("rows"))
    return jax.shard_map(
        local,
        mesh=mesh,
        in_specs=placed,
        out_specs=(P(("rows", "ctr")), P(("ctr", "rows"), None), P(("ctr", "rows"))),
        check_vma=False,
    )
```

time: 396 us -> 39.5 us (0.10)
  waiting for transfers between devices: 251 us -> 0 us
  blocking collectives: 108 us -> 0 us
  Pallas kernels: 0 us -> 32.8 us
  between operations: 17.6 us -> 0.65 us
  other arithmetic: 7.24 us -> 0 us
  matrix products: 5.72 us -> 0 us
    unnamed x3 -> x0, waiting for transfers between devices: 251 us -> none
    unnamed x1 -> x0, blocking collectives: 74.1 us -> none
    pmin x1 -> x0, blocking collectives: 34.4 us -> none  [local(): nearest = lax.pmin(partial_min, 'ctr')]
    pallas_call x0 -> x1, Pallas kernels: none -> 32.8 us  [local(): pl.pallas_call(functools.partial(kernel, n_rows, n_ctr), out_shape=(jax.S...]
    dot_general x4 -> x0, matrix products: 5.72 us -> none  [the longest x1 2.81 us: local(): lax.dot_general(member, weighted_points, (((0,), (0,)), ((), ())), prefer...]
    reduce_sum x3 -> x0, other arithmetic: 4.33 us -> none  [the longest x1 2.07 us: local(): point_norm = jnp.sum(jnp.square(points.astype(jnp.float32)), axis=1)]
  transfers between devices with their start and end apart: 2 -> 0, of which waited for: 1 -> 0; matrix products, arithmetic and copies ran while one was open for 2% -> 0% of each run, Pallas kernels for 0% -> 0%
where the time goes in v1:
time: 39.5 us; the launch traced here: 39.2 us
  Pallas kernels  32.8 us (83%)
  local copies, waits for them, and re-layouts  5.83 us (15%)
  between operations  0.65 us (2%)
    pallas_call x1, Pallas kernels, local(): pl.pallas_call(functools.partial(kernel, n_rows, n_ctr), out_shape=(jax.S...  32.8 us
    unnamed x11, local copies, waits for them, and re-layouts  5.83 us

profile of v1, /device:TPU:1, one launch (start us, length us, event | category | flops | bytes accessed | tf_op | source)
XLA Modules:
  0.0 39.2 jit_solution(13021503725065305549)
XLA Ops:
  0.6 0.0 copy-start
  0.6 1.6 %copy-done = bf16[1024,1024]{1,0:T(8,128)(2,1)S(1)} copy-done((bf16[1024,1024]{1,0:T(8,128)(2,1)S(1)}, bf16[1024,1024]{1,0:T(8,128)(2,1)}, u32[]{:S(2)}) %copy-start) | copy-done | bytes 2097176
  2.2 0.0 copy-start.1
  2.2 1.2 %copy-done.1 = bf16[512,1024]{1,0:T(8,128)(2,1)S(1)} copy-done((bf16[512,1024]{1,0:T(8,128)(2,1)S(1)}, bf16[512,1024]{1,0:T(8,128)(2,1)}, u32[]{:S(2)}) %copy-start.1) | copy-done | bytes 1048600
  3.4 0.0 copy-start.2
  3.5 0.7 %copy-done.2 = s32[1024]{0:T(1024)S(1)} copy-done((s32[1024]{0:T(1024)S(1)}, s32[1024]{0:T(1024)}, u32[]{:S(2)}) %copy-start.2) | copy-done | bytes 4120
  4.1 0.0 copy-start.3
  4.1 0.7 %copy-done.3 = f32[1024]{0:T(1024)S(1)} copy-done((f32[1024]{0:T(1024)S(1)}, f32[1024]{0:T(1024)}, u32[]{:S(2)}) %copy-start.3) | copy-done | bytes 4120
  4.8 32.8 %shard_map.67 = (f32[1,64]{1,0:T(1,128)S(1)}, f32[16,1024]{1,0:T(8,128)S(1)}, f32[1,16]{1,0:T(1,128)S(1)}) custom-call(bf16[1024,1024]{1,0:T(8,128)(2,1)S(1)} %copy-done, bf16[512,1024]{1,0:T(8,128)(2,1)S(1)} %copy-done.1, s32[8,128]{1,0:T(8,128)S(1)} %bitcast.4, f32[8,128]{1,0:T(8,128)S(1)} %bitcast.5), custom_call_target="tpu_custom_call" | custom-call | flops 1879048192 | bytes 3145728 | tf_op jit(solution)/shard_map/pallas_call | solution.py:276
  37.6 0.5 %copy.10 = f32[64]{0:T(128)} copy(f32[64]{0:T(128)S(1)} %bitcast.7) | data formatting | bytes 512
  38.1 0.6 %copy.11 = f32[16,1024]{1,0:T(8,128)} copy(f32[16,1024]{1,0:T(8,128)S(1)} %get-tuple-element.13) | data formatting | bytes 131072
  38.7 0.5 %copy.12 = f32[16]{0:T(128)} copy(f32[16]{0:T(128)S(1)} %bitcast.6) | data formatting | bytes 128
Async XLA Ops:
  0.6 1.6 %copy-start = (bf16[1024,1024]{1,0:T(8,128)(2,1)S(1)}, bf16[1024,1024]{1,0:T(8,128)(2,1)}, u32[]{:S(2)}) copy-start(bf16[1024,1024]{1,0:T(8,128)(2,1)} %points_hbm.1) | copy-start | bytes 6291460
  2.2 1.2 %copy-start.1 = (bf16[512,1024]{1,0:T(8,128)(2,1)S(1)}, bf16[512,1024]{1,0:T(8,128)(2,1)}, u32[]{:S(2)}) copy-start(bf16[512,1024]{1,0:T(8,128)(2,1)} %centers_hbm.1) | copy-start | bytes 3145732
  3.4 0.7 %copy-start.2 = (s32[1024]{0:T(1024)S(1)}, s32[1024]{0:T(1024)}, u32[]{:S(2)}) copy-start(s32[1024]{0:T(1024)} %param.6) | copy-start | bytes 12292
  4.1 0.7 %copy-start.3 = (f32[1024]{0:T(1024)S(1)}, f32[1024]{0:T(1024)}, u32[]{:S(2)}) copy-start(f32[1024]{0:T(1024)} %param.7) | copy-start | bytes 12292

commit v2 on v1

v2 whole, which is shorter than its diff:
```python
import functools

import jax
import jax.numpy as jnp
from jax import lax
from jax.experimental import pallas as pl
from jax.experimental.pallas import tpu as pltpu
from jax.sharding import PartitionSpec as P

KO = 16
CAP = 4
LANES = 128
MESH = pl.DeviceIdType.MESH
F32 = jnp.float32
BF16 = jnp.bfloat16
IDS = jnp.int16


def iota(shape, dim):
    return lax.broadcasted_iota(jnp.int32, shape, dim)


def dot_nt(a, b):
    return lax.dot_general(a, b, (((1,), (1,)), ((), ())), preferred_element_type=F32)


def dot_nn(a, b):
    return lax.dot_general(a, b, (((1,), (0,)), ((), ())), preferred_element_type=F32)


def split3(x):
    hi = x.astype(BF16).astype(F32)
    mid = (x - hi).astype(BF16).astype(F32)
    lo = ((x - hi) - mid).astype(BF16).astype(F32)
    return [hi, mid, lo]


def spread(parts):
    stack = jnp.concatenate(parts, axis=0)
    block = iota(stack.shape, 0) & 7
    return jnp.concatenate([jnp.where(block == b, stack, 0.0) for b in range(8)], axis=1).astype(BF16)


def kernel(
    n_rows,
    n_ctr,
    points_hbm,
    centers_hbm,
    assign_hbm,
    weight_hbm,
    row_share_ref,
    centroid_ref,
    share_ref,
    points,
    centers,
    assign_ref,
    weight_ref,
    pick,
    rows_out,
    rows_in,
    min_out,
    min_in,
    ids_out,
    ids_in,
    label_out,
    label_in,
    weight_out,
    weight_in,
    cost_out,
    cost_in,
    wide_ids,
    labels,
    near_ref,
    load_sem,
    send_sems,
    recv_sems,
    cost_sems,
):
    s = lax.axis_index("rows")
    c = lax.axis_index("ctr")
    chunk = points.shape[0] // 4
    n_own = row_share_ref.shape[1]

    def row_peer(d):
        k = d // 4
        away = ((k + 1) // 2) * (2 * (k % 2) - 1)
        low = lax.rem(s + d, 4)
        r = lax.rem(s // 4 + away + n_rows // 4, n_rows // 4) * 4 + low
        other = lax.rem(low // 2 + lax.rem(s, 4) // 2, 2)
        return r, c + other * (1 - 2 * lax.rem(c, 2))

    def row_peers(act):
        def step(d, carry):
            act(row_peer(n_rows - d))
            return carry

        lax.fori_loop(1, n_rows, step, 0)

    def ctr_peers(act):
        def step(d, carry):
            act(lax.rem(c + d, n_ctr))
            return carry

        lax.fori_loop(1, n_ctr, step, 0)

    barrier = pltpu.get_barrier_semaphore()
    ctr_peers(lambda p: pl.semaphore_signal(barrier, inc=1, device_id=(s, p), device_id_type=MESH))
    row_peers(lambda to: pl.semaphore_signal(barrier, inc=1, device_id=to, device_id_type=MESH))

    center_load = pltpu.make_async_copy(centers_hbm, centers, load_sem.at[4])
    center_load.start()
    point_loads = []
    for q in range(4):
        part = pl.ds(q * chunk, chunk)
        load = pltpu.make_async_copy(points_hbm.at[part], points.at[part], load_sem.at[q])
        load.start()
        point_loads.append(load)
    assign_load = pltpu.make_async_copy(assign_hbm, assign_ref, load_sem.at[5])
    assign_load.start()
    weight_load = pltpu.make_async_copy(weight_hbm, weight_ref, load_sem.at[6])
    weight_load.start()

    assign_load.wait()
    weight_load.wait()
    assign = assign_ref[...]
    weight = weight_ref[...]
    for h in range(2):
        ids_out[h] = assign[4 * h : 4 * h + 4].astype(IDS)
        weight_out[h] = weight[4 * h : 4 * h + 4]
    run = (assign >> 4) & (n_rows - 1)
    other = ((run >> 1) + lax.rem(s, 4) // 2) & 1
    run = jnp.where(assign >> 9 == c + other * (1 - 2 * lax.rem(c, 2)), run, -1)
    member = (assign & (KO - 1)).astype(F32)
    hot = [(run[b : b + 1, :] == iota((n_rows, LANES), 0)).astype(F32) for b in range(8)]
    before = jnp.concatenate(
        [
            (iota((LANES, LANES), 0) < iota((LANES, LANES), 1)).astype(F32),
            jnp.ones((LANES, LANES), F32),
        ],
        axis=1,
    ).astype(BF16)
    counted = dot_nn(jnp.concatenate(hot, axis=0).astype(BF16), before)
    carry = jnp.zeros((n_rows, LANES), F32)
    for b in range(8):
        rank = counted[b * n_rows : (b + 1) * n_rows, :LANES] + carry
        carry = carry + counted[b * n_rows : (b + 1) * n_rows, LANES:]
        rank = jnp.sum(hot[b] * rank, axis=0, keepdims=True).astype(jnp.int32)
        here = run[b : b + 1, :]
        code = jnp.where(here >= 0, here * CAP + rank, -1)
        lanes = pl.ds(b * LANES, LANES)
        pick[0:LANES, lanes] = (iota((LANES, LANES), 0) == code).astype(F32).astype(BF16)
        at = iota((2 * LANES, LANES), 0)
        at = (at >> 3) * CAP + (at & (CAP - 1))
        pick[LANES : 3 * LANES, lanes] = (at == code).astype(F32).astype(BF16)

    traits = spread([member + 1.0] + split3(weight))
    label_out[...] = jnp.sum(dot_nt(traits[0:8], pick[0:LANES, :]), axis=0, keepdims=True) - 1.0

    for load in point_loads:
        load.wait()
    row_weight = jnp.sum(dot_nt(pick[LANES : 3 * LANES, :], traits[8:32]), axis=1, keepdims=True)
    half = (iota((2 * LANES, 256), 0) >> 2) & 1
    tiles = []
    for t in range(2):
        low = dot_nn(pick[LANES : 3 * LANES, :], points[:, pl.ds(2 * t * 256, 256)])
        high = dot_nn(pick[LANES : 3 * LANES, :], points[:, pl.ds((2 * t + 1) * 256, 256)])
        tiles.append((jnp.where(half == 0, low, high) * row_weight).reshape(n_rows, 8, 256))
    rows_out[...] = jnp.concatenate(tiles, axis=1).astype(BF16)

    center_load.wait()
    wide = centers[...].astype(F32)
    half_norm = 0.5 * jnp.sum(wide * wide, axis=1, keepdims=True)
    for q in range(4):
        some = points[q * chunk : (q + 1) * chunk, :]
        wide = some.astype(F32)
        wide = wide * wide
        total = wide[:, 0:LANES]
        for k in range(1, 8):
            total = total + wide[:, k * LANES : (k + 1) * LANES]
        norm = jnp.sum(total.T, axis=0, keepdims=True)
        least = jnp.min(half_norm - dot_nt(centers[...], some), axis=0, keepdims=True)
        for k in range(2):
            min_out[2 * q + k : 2 * q + k + 1, :] = least[:, k * LANES : (k + 1) * LANES]
            near_ref[2 * q + k : 2 * q + k + 1, :] = norm[:, k * LANES : (k + 1) * LANES]

    side = iota((LANES, LANES), 0) == iota((LANES, LANES), 1)
    own = assign_ref[pl.ds(c // 2, 1), :].astype(F32)
    own = jnp.sum(jnp.where(side, own, 0.0), axis=1, keepdims=True)
    own = jnp.where(c % 2 == 0, own[:n_own], own[n_own : 2 * n_own])
    first = (c * n_rows + s) * KO
    own = jnp.concatenate([own.astype(jnp.int32), first + iota((KO, 1), 0)], axis=0)
    own = jnp.broadcast_to(own, (n_own + KO, LANES))

    pl.semaphore_wait(barrier, n_rows + n_ctr - 2)

    def copy(src, dst, i, recv, device):
        return pltpu.make_async_remote_copy(
            src, dst, send_sems.at[i], recv, device_id=device, device_id_type=MESH
        )

    def wait_all(ref, count, sem):
        whole = ref.at[pl.ds(0, count)]
        pltpu.make_async_copy(whole, whole, sem).wait()

    ctr_peers(lambda p: copy(min_out, min_in.at[c], 0, recv_sems.at[0], (s, p)).start())
    def send_half(src, dst, i):
        def send(to):
            h = lax.rem(to[0], 2)
            copy(src.at[h], dst.at[h, s], i, recv_sems.at[i], to).start()

        row_peers(send)

    core = lax.rem(s, 2)
    send_half(ids_out, ids_in, 1)
    send_half(weight_out, weight_in, 2)
    row_peers(lambda to: copy(label_out, label_in.at[s], 3, recv_sems.at[3], to).start())
    row_peers(lambda to: copy(rows_out.at[to[0]], rows_in.at[s], 4, recv_sems.at[4], to).start())
    min_in[c] = min_out[...]
    ids_in[core, s] = ids_out[core]
    weight_in[core, s] = weight_out[core]
    label_in[s] = label_out[...]
    rows_in[s] = rows_out[s]

    wait_all(min_in, n_ctr - 1, recv_sems.at[0])
    near = near_ref[...] + 2.0 * jnp.min(min_in[...], axis=0)
    near_ref[...] = near
    cost_out[...] = near * weight
    row_peers(lambda to: copy(cost_out, cost_in.at[s], 5, cost_sems.at[s], to).start())
    cost_in[s] = near * weight

    def add(r, values, sums):
        total, each = sums
        ids = wide_ids[r]
        for b in range(8):
            each = each + jnp.where(ids[b : b + 1, :] == own, values[b : b + 1, :], 0.0)
        return total + values, each

    zeros = (jnp.zeros((8, LANES), F32), jnp.zeros(own.shape, F32))

    def add_weight(r, sums):
        for h in range(2):
            wide_ids[r, 4 * h : 4 * h + 4] = ids_in[h, r].astype(jnp.int32)
        return add(r, jnp.concatenate([weight_in[0, r], weight_in[1, r]], axis=0), sums)

    wait_all(ids_in.at[0], n_rows - 1, recv_sems.at[1])
    wait_all(weight_in.at[0], n_rows - 1, recv_sems.at[2])
    partner = (s + 1 - 2 * core, c)
    give = [
        copy(ids_in.at[core], ids_in.at[core], 6, recv_sems.at[5], partner),
        copy(weight_in.at[core], weight_in.at[core], 7, recv_sems.at[6], partner),
    ]
    for one in give:
        one.start()
    for one in give:
        one.wait_recv()
    weight_sum, size = lax.fori_loop(0, n_rows, add_weight, zeros)
    weight_sum = jnp.sum(weight_sum, keepdims=True)
    size = jnp.maximum(jnp.sum(size, axis=1, keepdims=True), 1.0)

    wait_all(label_in, n_rows - 1, recv_sems.at[3])
    for r in range(n_rows):
        labels[r : r + 1, :] = label_in[r]
    lane = iota((LANES, n_rows * KO), 1)
    at = iota((LANES, n_rows * KO), 0)
    place = (at == s * CAP + (lane & (CAP - 1))).astype(F32).astype(BF16)
    ids = dot_nn(labels[...].astype(BF16), place)
    slab = iota((n_rows, n_rows * KO), 0) == iota((n_rows, n_rows * KO), 1) // KO
    ids = jnp.sum(jnp.where(slab, ids, 0.0), axis=0, keepdims=True).astype(jnp.int32)
    at = iota((4 * KO, n_rows * KO), 0)
    quarter = (iota((4 * KO, n_rows * KO), 1) & (KO - 1)) >> 2
    member = ((at & (KO - 1)) == ids) & ((at >> 4) == quarter)
    member = member.astype(F32).astype(BF16)
    wait_all(rows_in, n_rows - 1, recv_sems.at[4])
    coord = dot_nn(member, rows_in[...].reshape(n_rows * KO, 256))
    for q in range(4):
        centroid_ref[:, q * 256 : (q + 1) * 256] = coord[q * KO : (q + 1) * KO, :] / size[n_own:]

    def add_cost(d, sums):
        r, _ = row_peer(d)
        pltpu.make_async_copy(cost_in.at[r], cost_in.at[r], cost_sems.at[r]).wait()
        return add(r, cost_in[r], sums)

    cost_sum, cost = lax.fori_loop(1, n_rows, add_cost, add(s, cost_in[s], zeros))
    mean = jnp.sum(cost_sum, keepdims=True) / weight_sum
    share = jnp.sum(cost, axis=1, keepdims=True) / (size * mean)
    diagonal = iota(own.shape, 0) == iota(own.shape, 1)
    share = jnp.sum(jnp.where(diagonal, share, 0.0), axis=0, keepdims=True)
    share_ref[...] = share[:, n_own : n_own + KO]
    near = near_ref[pl.ds(c // 2, 1), :]
    near = jnp.where(c % 2 == 0, near[:, :n_own], near[:, n_own : 2 * n_own])
    row_share_ref[...] = near / mean + 2.0 * share[:, :n_own]

    wait_all(min_in, n_ctr - 1, send_sems.at[0])
    wait_all(ids_in.at[0], n_rows - 1, send_sems.at[1])
    wait_all(weight_in.at[0], n_rows - 1, send_sems.at[2])
    for one in give:
        one.wait_send()
    wait_all(label_in, n_rows - 1, send_sems.at[3])
    wait_all(rows_in, n_rows - 1, send_sems.at[4])
    wait_all(cost_in, n_rows - 1, send_sems.at[5])


def deliver(*refs):
    n = len(refs) // 2
    for i in range(n):
        refs[n + i][...] = refs[i][...]


def local(points, centers, assignment, row_weight):
    slab_rows, width = points.shape
    block = centers.shape[0]
    n_rows = lax.axis_size("rows")
    n_ctr = lax.axis_size("ctr")
    vmem = pl.BlockSpec(memory_space=pltpu.VMEM)
    hbm = pl.BlockSpec(memory_space=pltpu.HBM)
    row_share, centroid, share = pl.pallas_call(
        functools.partial(kernel, n_rows, n_ctr),
        out_shape=(
            jax.ShapeDtypeStruct((1, slab_rows // n_ctr), F32),
            jax.ShapeDtypeStruct((KO, width), F32),
            jax.ShapeDtypeStruct((1, KO), F32),
        ),
        in_specs=[hbm, hbm, hbm, hbm],
        out_specs=(vmem, vmem, vmem),
        scratch_shapes=[
            pltpu.VMEM((slab_rows, width), BF16),
            pltpu.VMEM((block, width), BF16),
            pltpu.VMEM((8, LANES), jnp.int32),
            pltpu.VMEM((8, LANES), F32),
            pltpu.VMEM((3 * LANES, slab_rows), BF16),
            pltpu.VMEM((n_rows, 16, 256), BF16),
            pltpu.VMEM((n_rows, 16, 256), BF16),
            pltpu.VMEM((8, LANES), F32),
            pltpu.VMEM((n_ctr, 8, LANES), F32),
            pltpu.VMEM((2, 4, LANES), IDS),
            pltpu.VMEM((2, n_rows, 4, LANES), IDS),
            pltpu.VMEM((1, LANES), F32),
            pltpu.VMEM((n_rows, 1, LANES), F32),
            pltpu.VMEM((2, 4, LANES), F32),
            pltpu.VMEM((2, n_rows, 4, LANES), F32),
            pltpu.VMEM((8, LANES), F32),
            pltpu.VMEM((n_rows, 8, LANES), F32),
            pltpu.VMEM((n_rows, 8, LANES), jnp.int32),
            pltpu.VMEM((n_rows, LANES), F32),
            pltpu.VMEM((8, LANES), F32),
            pltpu.SemaphoreType.DMA((7,)),
            pltpu.SemaphoreType.DMA((8,)),
            pltpu.SemaphoreType.DMA((7,)),
            pltpu.SemaphoreType.DMA((n_rows,)),
        ],
        compiler_params=pltpu.CompilerParams(
            collective_id=0, has_side_effects=True
        ),
        cost_estimate=pl.CostEstimate(
            flops=2 * slab_rows * width * (block + 3 * LANES),
            bytes_accessed=2 * (slab_rows + block) * width,
            transcendentals=0,
        ),
    )(points, centers, assignment.reshape(8, LANES), row_weight.reshape(8, LANES))
    made = (row_share, centroid, share)
    row_share, centroid, share = pl.pallas_call(
        deliver,
        out_shape=tuple(jax.ShapeDtypeStruct(x.shape, x.dtype) for x in made),
        in_specs=[vmem] * 3,
        out_specs=(vmem,) * 3,
    )(*made)
    return row_share.reshape(-1), centroid, share.reshape(-1)


def solution(mesh):
    placed = (P("rows", None), P("ctr", None), P("rows"), P("rows"))
    return jax.shard_map(
        local,
        mesh=mesh,
        in_specs=placed,
        out_specs=(P(("rows", "ctr")), P(("ctr", "rows"), None), P(("ctr", "rows"))),
        check_vma=False,
    )
```

time: 39.5 us -> 33.8 us (0.86)
  local copies, waits for them, and re-layouts: 5.83 us -> 0 us
    unnamed x11 -> x0, local copies, waits for them, and re-layouts: 5.83 us -> none
    pallas_call x0 -> x1, Pallas kernels: none -> 1.48 us  [local(): pl.pallas_call(deliver, out_shape=tuple((jax.ShapeDtypeStruct(x.shape, x....]
    pallas_call x1, Pallas kernels: 32.8 us -> 31.5 us  [local(): pl.pallas_call(functools.partial(kernel, n_rows, n_ctr), out_shape=(jax.S...]
where the time goes in v2:
time: 33.8 us; the launch traced here: 33.7 us
  Pallas kernels  33 us (98%)
  between operations  0.64 us (2%)
    pallas_call x1, Pallas kernels, local(): pl.pallas_call(functools.partial(kernel, n_rows, n_ctr), out_shape=(jax.S...  31.5 us
    pallas_call x1, Pallas kernels, local(): pl.pallas_call(deliver, out_shape=tuple((jax.ShapeDtypeStruct(x.shape, x....  1.48 us

profile of v2, /device:TPU:1, one launch (start us, length us, event | category | flops | bytes accessed | tf_op | source)
XLA Modules:
  0.0 33.7 jit_solution(14797091029507625319)
XLA Ops:
  0.6 31.5 %shard_map.67 = (f32[1,64]{1,0:T(1,128)}, f32[16,1024]{1,0:T(8,128)}, f32[1,16]{1,0:T(1,128)}) custom-call(bf16[1024,1024]{1,0:T(8,128)(2,1)} %points_hbm.1, bf16[512,1024]{1,0:T(8,128)(2,1)} %centers_hbm.1, s32[8,128]{1,0:T(8,128)} %bitcast.4, f32[8,128]{1,0:T(8,128)} %bitcast.5), custom_call_target="tpu_custom_call" | custom-call | flops 1879048192 | bytes 3145728 | tf_op jit(solution)/shard_map/pallas_call | solution.py:316
  32.2 1.5 %shard_map.68 = (f32[1,64]{1,0:T(1,128)}, f32[16,1024]{1,0:T(8,128)}, f32[1,16]{1,0:T(1,128)}) custom-call(f32[1,64]{1,0:T(1,128)} %get-tuple-element.9.refs_0_, f32[16,1024]{1,0:T(8,128)} %get-tuple-element.10.refs_1_, f32[1,16]{1,0:T(1,128)} %get-tuple-element.11.refs_2_), custom_call_target="tpu_custom_call" | custom-call | tf_op jit(solution)/shard_map/pallas_call | solution.py:361

commit v3 on v2

--- a/solution.py
+++ b/solution.py
@@ -75,6 +75,8 @@
     send_sems,
     recv_sems,
     cost_sems,
+    late_sem,
+    go_sem,
 ):
     s = lax.axis_index("rows")
     c = lax.axis_index("ctr")
@@ -82,30 +84,42 @@
     n_own = row_share_ref.shape[1]
 
     def row_peer(d):
-        k = d // 4
-        away = ((k + 1) // 2) * (2 * (k % 2) - 1)
-        low = lax.rem(s + d, 4)
-        r = lax.rem(s // 4 + away + n_rows // 4, n_rows // 4) * 4 + low
-        other = lax.rem(low // 2 + lax.rem(s, 4) // 2, 2)
-        return r, c + other * (1 - 2 * lax.rem(c, 2))
-
-    def row_peers(act):
+        k = d >> 2
+        away = ((k + 1) >> 1) * (2 * (k & 1) - 1)
+        low = (s + d) & 3
+        r = (((s >> 2) + away) & (n_rows // 4 - 1)) * 4 + low
+        other = ((low >> 1) + (s >> 1)) & 1
+        return r, c + other * (1 - 2 * (c & 1))
+
+    def row_peers(act, unroll=False):
+        if unroll:
+            for d in range(n_rows - 1, 0, -1):
+                act(row_peer(d))
+            return
+
         def step(d, carry):
             act(row_peer(n_rows - d))
             return carry
 
         lax.fori_loop(1, n_rows, step, 0)
 
-    def ctr_peers(act):
-        def step(d, carry):
-            act(lax.rem(c + d, n_ctr))
-            return carry
-
-        lax.fori_loop(1, n_ctr, step, 0)
+    half = n_ctr // 2
+
+    def early_peers(act):
+        for d in sorted(range(half), key=lambda d: abs(2 * d - half)):
+            p = (c + d) & (half - 1)
+            pl.when(p != c)(functools.partial(act, p))
+
+    def late_peers(act):
+        for d in range(half):
+            p = half + ((c + d) & (half - 1))
+            pl.when(p != c)(functools.partial(act, p))
 
     barrier = pltpu.get_barrier_semaphore()
-    ctr_peers(lambda p: pl.semaphore_signal(barrier, inc=1, device_id=(s, p), device_id_type=MESH))
-    row_peers(lambda to: pl.semaphore_signal(barrier, inc=1, device_id=to, device_id_type=MESH))
+    assign_load = pltpu.make_async_copy(assign_hbm, assign_ref, load_sem.at[5])
+    assign_load.start()
+    weight_load = pltpu.make_async_copy(weight_hbm, weight_ref, load_sem.at[6])
+    weight_load.start()
 
     center_load = pltpu.make_async_copy(centers_hbm, centers, load_sem.at[4])
     center_load.start()
@@ -115,10 +129,16 @@
         load = pltpu.make_async_copy(points_hbm.at[part], points.at[part], load_sem.at[q])
         load.start()
         point_loads.append(load)
-    assign_load = pltpu.make_async_copy(assign_hbm, assign_ref, load_sem.at[5])
-    assign_load.start()
-    weight_load = pltpu.make_async_copy(weight_hbm, weight_ref, load_sem.at[6])
-    weight_load.start()
+
+    def enter(p):
+        pl.semaphore_signal(barrier, inc=1, device_id=(s, p), device_id_type=MESH)
+
+    @pl.when(c < half)
+    def _():
+        early_peers(enter)
+        late_peers(enter)
+
+    row_peers(lambda to: pl.semaphore_signal(barrier, inc=1, device_id=to, device_id_type=MESH), True)
 
     assign_load.wait()
     weight_load.wait()
@@ -158,15 +178,6 @@
 
     for load in point_loads:
         load.wait()
-    row_weight = jnp.sum(dot_nt(pick[LANES : 3 * LANES, :], traits[8:32]), axis=1, keepdims=True)
-    half = (iota((2 * LANES, 256), 0) >> 2) & 1
-    tiles = []
-    for t in range(2):
-        low = dot_nn(pick[LANES : 3 * LANES, :], points[:, pl.ds(2 * t * 256, 256)])
-        high = dot_nn(pick[LANES : 3 * LANES, :], points[:, pl.ds((2 * t + 1) * 256, 256)])
-        tiles.append((jnp.where(half == 0, low, high) * row_weight).reshape(n_rows, 8, 256))
-    rows_out[...] = jnp.concatenate(tiles, axis=1).astype(BF16)
-
     center_load.wait()
     wide = centers[...].astype(F32)
     half_norm = 0.5 * jnp.sum(wide * wide, axis=1, keepdims=True)
@@ -183,6 +194,15 @@
             min_out[2 * q + k : 2 * q + k + 1, :] = least[:, k * LANES : (k + 1) * LANES]
             near_ref[2 * q + k : 2 * q + k + 1, :] = norm[:, k * LANES : (k + 1) * LANES]
 
+    row_weight = jnp.sum(dot_nt(pick[LANES : 3 * LANES, :], traits[8:32]), axis=1, keepdims=True)
+    odd = (iota((2 * LANES, 256), 0) >> 2) & 1
+    tiles = []
+    for t in range(2):
+        low = dot_nn(pick[LANES : 3 * LANES, :], points[:, pl.ds(2 * t * 256, 256)])
+        high = dot_nn(pick[LANES : 3 * LANES, :], points[:, pl.ds((2 * t + 1) * 256, 256)])
+        tiles.append((jnp.where(odd == 0, low, high) * row_weight).reshape(n_rows, 8, 256))
+    rows_out[...] = jnp.concatenate(tiles, axis=1).astype(BF16)
+
     side = iota((LANES, LANES), 0) == iota((LANES, LANES), 1)
     own = assign_ref[pl.ds(c // 2, 1), :].astype(F32)
     own = jnp.sum(jnp.where(side, own, 0.0), axis=1, keepdims=True)
@@ -191,7 +211,7 @@
     own = jnp.concatenate([own.astype(jnp.int32), first + iota((KO, 1), 0)], axis=0)
     own = jnp.broadcast_to(own, (n_own + KO, LANES))
 
-    pl.semaphore_wait(barrier, n_rows + n_ctr - 2)
+    pl.semaphore_wait(barrier, n_rows + half - 2 + c // half)
 
     def copy(src, dst, i, recv, device):
         return pltpu.make_async_remote_copy(
@@ -202,15 +222,26 @@
         whole = ref.at[pl.ds(0, count)]
         pltpu.make_async_copy(whole, whole, sem).wait()
 
-    ctr_peers(lambda p: copy(min_out, min_in.at[c], 0, recv_sems.at[0], (s, p)).start())
+    def send_min(p):
+        copy(min_out, min_in.at[c], 0, recv_sems.at[0], (s, p)).start()
+
+    def tell_late(p):
+        pl.semaphore_signal(late_sem, inc=1, device_id=(s, p), device_id_type=MESH)
+
+    early_peers(send_min)
+
+    @pl.when(c >= half)
+    def _():
+        early_peers(tell_late)
+
     def send_half(src, dst, i):
         def send(to):
-            h = lax.rem(to[0], 2)
+            h = to[0] & 1
             copy(src.at[h], dst.at[h, s], i, recv_sems.at[i], to).start()
 
         row_peers(send)
 
-    core = lax.rem(s, 2)
+    core = s & 1
     send_half(ids_out, ids_in, 1)
     send_half(weight_out, weight_in, 2)
     row_peers(lambda to: copy(label_out, label_in.at[s], 3, recv_sems.at[3], to).start())
@@ -221,12 +252,24 @@
     label_in[s] = label_out[...]
     rows_in[s] = rows_out[s]
 
+    @pl.when(c >= half)
+    def _():
+        pl.semaphore_wait(go_sem, 1)
+        late_peers(send_min)
+
     wait_all(min_in, n_ctr - 1, recv_sems.at[0])
     near = near_ref[...] + 2.0 * jnp.min(min_in[...], axis=0)
     near_ref[...] = near
     cost_out[...] = near * weight
-    row_peers(lambda to: copy(cost_out, cost_in.at[s], 5, cost_sems.at[s], to).start())
+    row_peers(lambda to: copy(cost_out, cost_in.at[s], 5, cost_sems.at[s], to).start(), True)
     cost_in[s] = near * weight
+
+    @pl.when(c < half)
+    def _():
+        pl.semaphore_wait(late_sem, half)
+        mirror = n_ctr - 2 - 2 * (c // 2) + c % 2
+        pl.semaphore_signal(go_sem, inc=1, device_id=(s, mirror), device_id_type=MESH)
+        late_peers(send_min)
 
     def add(r, values, sums):
         total, each = sums
@@ -347,6 +390,8 @@
             pltpu.SemaphoreType.DMA((8,)),
             pltpu.SemaphoreType.DMA((7,)),
             pltpu.SemaphoreType.DMA((n_rows,)),
+            pltpu.SemaphoreType.REGULAR,
+            pltpu.SemaphoreType.REGULAR,
         ],
         compiler_params=pltpu.CompilerParams(
             collective_id=0, has_side_effects=True

time: 33.8 us -> 30.7 us (0.908)
  Pallas kernels: 33 us -> 29.9 us
    pallas_call x1, Pallas kernels: 31.5 us -> 28.4 us  [local(): pl.pallas_call(functools.partial(kernel, n_rows, n_ctr), out_shape=(jax.S...]
where the time goes in v3:
time: 30.7 us; the launch traced here: 30.5 us
  Pallas kernels  29.9 us (97%)
  between operations  0.64 us (2%)
    pallas_call x1, Pallas kernels, local(): pl.pallas_call(functools.partial(kernel, n_rows, n_ctr), out_shape=(jax.S...  28.4 us
    pallas_call x1, Pallas kernels, local(): pl.pallas_call(deliver, out_shape=tuple((jax.ShapeDtypeStruct(x.shape, x....  1.48 us

profile of v3, /device:TPU:1, one launch (start us, length us, event | category | flops | bytes accessed | tf_op | source)
XLA Modules:
  0.0 30.5 jit_solution(15403763374599224466)
XLA Ops:
  0.6 28.4 %shard_map.67 = (f32[1,64]{1,0:T(1,128)}, f32[16,1024]{1,0:T(8,128)}, f32[1,16]{1,0:T(1,128)}) custom-call(bf16[1024,1024]{1,0:T(8,128)(2,1)} %points_hbm.1, bf16[512,1024]{1,0:T(8,128)(2,1)} %centers_hbm.1, s32[8,128]{1,0:T(8,128)} %bitcast.4, f32[8,128]{1,0:T(8,128)} %bitcast.5), custom_call_target="tpu_custom_call" | custom-call | flops 1879048192 | bytes 3145728 | tf_op jit(solution)/shard_map/pallas_call | solution.py:359
  29.0 1.5 %shard_map.68 = (f32[1,64]{1,0:T(1,128)}, f32[16,1024]{1,0:T(8,128)}, f32[1,16]{1,0:T(1,128)}) custom-call(f32[1,64]{1,0:T(1,128)} %get-tuple-element.9.refs_0_, f32[16,1024]{1,0:T(8,128)} %get-tuple-element.10.refs_1_, f32[1,16]{1,0:T(1,128)} %get-tuple-element.11.refs_2_), custom_call_target="tpu_custom_call" | custom-call | tf_op jit(solution)/shard_map/pallas_call | solution.py:406

commit v4 on v3

--- a/solution.py
+++ b/solution.py
@@ -13,7 +13,7 @@
 MESH = pl.DeviceIdType.MESH
 F32 = jnp.float32
 BF16 = jnp.bfloat16
-IDS = jnp.int16
+CODE = jnp.int16
 
 
 def iota(shape, dim):
@@ -33,6 +33,23 @@
     mid = (x - hi).astype(BF16).astype(F32)
     lo = ((x - hi) - mid).astype(BF16).astype(F32)
     return [hi, mid, lo]
+
+
+def weight_code(x):
+    return (((x - 0.25) * (65535 / 3.75) + 0.5).astype(jnp.int32) - 32768).astype(CODE)
+
+
+def code_weight(code):
+    return (code.astype(jnp.int32) + 32768).astype(F32) * (3.75 / 65535) + 0.25
+
+
+def cost_code(x):
+    at = (jnp.log2(jnp.maximum(x, 2.0**-106)) + 106.0) * 512.0 + 0.5
+    return (jnp.minimum(at, 65535.0).astype(jnp.int32) - 32768).astype(CODE)
+
+
+def code_cost(code):
+    return jnp.exp2((code.astype(jnp.int32) + 32768).astype(F32) * (1 / 512) - 106.0)
 
 
 def spread(parts):
@@ -64,8 +81,6 @@
     ids_in,
     label_out,
     label_in,
-    weight_out,
-    weight_in,
     cost_out,
     cost_in,
     wide_ids,
@@ -140,44 +155,56 @@
 
     row_peers(lambda to: pl.semaphore_signal(barrier, inc=1, device_id=to, device_id_type=MESH), True)
 
+    def slots():
+        assign = assign_ref[...]
+        weight = weight_ref[...]
+        for h in range(2):
+            ids_out[h, 0] = assign[4 * h : 4 * h + 4].astype(CODE)
+            ids_out[h, 1] = weight_code(weight[4 * h : 4 * h + 4])
+        run = (assign >> 4) & (n_rows - 1)
+        other = ((run >> 1) + lax.rem(s, 4) // 2) & 1
+        run = jnp.where(assign >> 9 == c + other * (1 - 2 * lax.rem(c, 2)), run, -1)
+        member = (assign & (KO - 1)).astype(F32)
+        hot = [(run[b : b + 1, :] == iota((n_rows, LANES), 0)).astype(F32) for b in range(8)]
+        before = jnp.concatenate(
+            [
+                (iota((LANES, LANES), 0) < iota((LANES, LANES), 1)).astype(F32),
+                jnp.ones((LANES, LANES), F32),
+            ],
+            axis=1,
+        ).astype(BF16)
+        counted = dot_nn(jnp.concatenate(hot, axis=0).astype(BF16), before)
+        carry = jnp.zeros((n_rows, LANES), F32)
+        for b in range(8):
+            rank = counted[b * n_rows : (b + 1) * n_rows, :LANES] + carry
+            carry = carry + counted[b * n_rows : (b + 1) * n_rows, LANES:]
+            rank = jnp.sum(hot[b] * rank, axis=0, keepdims=True).astype(jnp.int32)
+            here = run[b : b + 1, :]
+            code = jnp.where(here >= 0, here * CAP + rank, -1)
+            lanes = pl.ds(b * LANES, LANES)
+            pick[0:LANES, lanes] = (iota((LANES, LANES), 0) == code).astype(F32).astype(BF16)
+            at = iota((2 * LANES, LANES), 0)
+            at = (at >> 3) * CAP + (at & (CAP - 1))
+            pick[LANES : 3 * LANES, lanes] = (at == code).astype(F32).astype(BF16)
+
+        traits = spread([member + 1.0] + split3(weight))
+        label_out[...] = jnp.sum(dot_nt(traits[0:8], pick[0:LANES, :]), axis=0, keepdims=True) - 1.0
+
+        row_weight = jnp.sum(dot_nt(pick[LANES : 3 * LANES, :], traits[8:32]), axis=1, keepdims=True)
+        odd = (iota((2 * LANES, 256), 0) >> 2) & 1
+        tiles = []
+        for t in range(2):
+            low = dot_nn(pick[LANES : 3 * LANES, :], points[:, pl.ds(2 * t * 256, 256)])
+            high = dot_nn(pick[LANES : 3 * LANES, :], points[:, pl.ds((2 * t + 1) * 256, 256)])
+            tiles.append((jnp.where(odd == 0, low, high) * row_weight).reshape(n_rows, 8, 256))
+        rows_out[...] = jnp.concatenate(tiles, axis=1).astype(BF16)
+
     assign_load.wait()
     weight_load.wait()
-    assign = assign_ref[...]
-    weight = weight_ref[...]
-    for h in range(2):
-        ids_out[h] = assign[4 * h : 4 * h + 4].astype(IDS)
-        weight_out[h] = weight[4 * h : 4 * h + 4]
-    run = (assign >> 4) & (n_rows - 1)
-    other = ((run >> 1) + lax.rem(s, 4) // 2) & 1
-    run = jnp.where(assign >> 9 == c + other * (1 - 2 * lax.rem(c, 2)), run, -1)
-    member = (assign & (KO - 1)).astype(F32)
-    hot = [(run[b : b + 1, :] == iota((n_rows, LANES), 0)).astype(F32) for b in range(8)]
-    before = jnp.concatenate(
-        [
-            (iota((LANES, LANES), 0) < iota((LANES, LANES), 1)).astype(F32),
-            jnp.ones((LANES, LANES), F32),
-        ],
-        axis=1,
-    ).astype(BF16)
-    counted = dot_nn(jnp.concatenate(hot, axis=0).astype(BF16), before)
-    carry = jnp.zeros((n_rows, LANES), F32)
-    for b in range(8):
-        rank = counted[b * n_rows : (b + 1) * n_rows, :LANES] + carry
-        carry = carry + counted[b * n_rows : (b + 1) * n_rows, LANES:]
-        rank = jnp.sum(hot[b] * rank, axis=0, keepdims=True).astype(jnp.int32)
-        here = run[b : b + 1, :]
-        code = jnp.where(here >= 0, here * CAP + rank, -1)
-        lanes = pl.ds(b * LANES, LANES)
-        pick[0:LANES, lanes] = (iota((LANES, LANES), 0) == code).astype(F32).astype(BF16)
-        at = iota((2 * LANES, LANES), 0)
-        at = (at >> 3) * CAP + (at & (CAP - 1))
-        pick[LANES : 3 * LANES, lanes] = (at == code).astype(F32).astype(BF16)
-
-    traits = spread([member + 1.0] + split3(weight))
-    label_out[...] = jnp.sum(dot_nt(traits[0:8], pick[0:LANES, :]), axis=0, keepdims=True) - 1.0
-
     for load in point_loads:
         load.wait()
+    pl.when(c < half)(slots)
+
     center_load.wait()
     wide = centers[...].astype(F32)
     half_norm = 0.5 * jnp.sum(wide * wide, axis=1, keepdims=True)
@@ -194,14 +221,65 @@
             min_out[2 * q + k : 2 * q + k + 1, :] = least[:, k * LANES : (k + 1) * LANES]
             near_ref[2 * q + k : 2 * q + k + 1, :] = norm[:, k * LANES : (k + 1) * LANES]
 
-    row_weight = jnp.sum(dot_nt(pick[LANES : 3 * LANES, :], traits[8:32]), axis=1, keepdims=True)
-    odd = (iota((2 * LANES, 256), 0) >> 2) & 1
-    tiles = []
-    for t in range(2):
-        low = dot_nn(pick[LANES : 3 * LANES, :], points[:, pl.ds(2 * t * 256, 256)])
-        high = dot_nn(pick[LANES : 3 * LANES, :], points[:, pl.ds((2 * t + 1) * 256, 256)])
-        tiles.append((jnp.where(odd == 0, low, high) * row_weight).reshape(n_rows, 8, 256))
-    rows_out[...] = jnp.concatenate(tiles, axis=1).astype(BF16)
+    pl.semaphore_wait(barrier, n_rows + half - 2 + c // half)
+
+    def copy(src, dst, i, recv, device):
+        return pltpu.make_async_remote_copy(
+            src, dst, send_sems.at[i], recv, device_id=device, device_id_type=MESH
+        )
+
+    def wait_all(ref, count, sem):
+        whole = ref.at[pl.ds(0, count)]
+        pltpu.make_async_copy(whole, whole, sem).wait()
+
+    def send_min(p):
+        copy(min_out, min_in.at[c], 0, recv_sems.at[0], (s, p)).start()
+
+    def tell_late(p):
+        pl.semaphore_signal(late_sem, inc=1, device_id=(s, p), device_id_type=MESH)
+
+    early_peers(send_min)
+
+    @pl.when(c >= half)
+    def _():
+        early_peers(tell_late)
+        slots()
+
+    def send_half(src, dst, i):
+        def send(to):
+            h = to[0] & 1
+            copy(src.at[h], dst.at[h, s], i, recv_sems.at[i], to).start()
+
+        row_peers(send)
+
+    core = s & 1
+    send_half(ids_out, ids_in, 1)
+    row_peers(lambda to: copy(label_out, label_in.at[s], 3, recv_sems.at[3], to).start())
+    row_peers(lambda to: copy(rows_out.at[to[0]], rows_in.at[s], 4, recv_sems.at[4], to).start())
+    min_in[c] = min_out[...]
+    ids_in[core, s] = ids_out[core]
+    label_in[s] = label_out[...]
+    rows_in[s] = rows_out[s]
+
+    @pl.when(c < half)
+    def _():
+        pl.semaphore_wait(late_sem, half)
+        mirror = n_ctr - 2 - 2 * (c // 2) + c % 2
+        pl.semaphore_signal(go_sem, inc=1, device_id=(s, mirror), device_id_type=MESH)
+        late_peers(send_min)
+
+    @pl.when(c >= half)
+    def _():
+        pl.semaphore_wait(go_sem, 1)
+        late_peers(send_min)
+
+    wait_all(min_in, n_ctr - 1, recv_sems.at[0])
+    near = near_ref[...] + 2.0 * jnp.min(min_in[...], axis=0)
+    near_ref[...] = near
+    cost = near * weight_ref[...]
+    cost_out[...] = cost_code(cost)
+    row_peers(lambda to: copy(cost_out, cost_in.at[s], 5, cost_sems.at[s], to).start(), True)
+    cost_in[s] = cost_out[...]
 
     side = iota((LANES, LANES), 0) == iota((LANES, LANES), 1)
     own = assign_ref[pl.ds(c // 2, 1), :].astype(F32)
@@ -211,66 +289,6 @@
     own = jnp.concatenate([own.astype(jnp.int32), first + iota((KO, 1), 0)], axis=0)
     own = jnp.broadcast_to(own, (n_own + KO, LANES))
 
-    pl.semaphore_wait(barrier, n_rows + half - 2 + c // half)
-
-    def copy(src, dst, i, recv, device):
-        return pltpu.make_async_remote_copy(
-            src, dst, send_sems.at[i], recv, device_id=device, device_id_type=MESH
-        )
-
-    def wait_all(ref, count, sem):
-        whole = ref.at[pl.ds(0, count)]
-        pltpu.make_async_copy(whole, whole, sem).wait()
-
-    def send_min(p):
-        copy(min_out, min_in.at[c], 0, recv_sems.at[0], (s, p)).start()
-
-    def tell_late(p):
-        pl.semaphore_signal(late_sem, inc=1, device_id=(s, p), device_id_type=MESH)
-
-    early_peers(send_min)
-
-    @pl.when(c >= half)
-    def _():
-        early_peers(tell_late)
-
-    def send_half(src, dst, i):
-        def send(to):
-            h = to[0] & 1
-            copy(src.at[h], dst.at[h, s], i, recv_sems.at[i], to).start()
-
-        row_peers(send)
-
-    core = s & 1
-    send_half(ids_out, ids_in, 1)
-    send_half(weight_out, weight_in, 2)
-    row_peers(lambda to: copy(label_out, label_in.at[s], 3, recv_sems.at[3], to).start())
-    row_peers(lambda to: copy(rows_out.at[to[0]], rows_in.at[s], 4, recv_sems.at[4], to).start())
-    min_in[c] = min_out[...]
-    ids_in[core, s] = ids_out[core]
-    weight_in[core, s] = weight_out[core]
-    label_in[s] = label_out[...]
-    rows_in[s] = rows_out[s]
-
-    @pl.when(c >= half)
-    def _():
-        pl.semaphore_wait(go_sem, 1)
-        late_peers(send_min)
-
-    wait_all(min_in, n_ctr - 1, recv_sems.at[0])
-    near = near_ref[...] + 2.0 * jnp.min(min_in[...], axis=0)
-    near_ref[...] = near
-    cost_out[...] = near * weight
-    row_peers(lambda to: copy(cost_out, cost_in.at[s], 5, cost_sems.at[s], to).start(), True)
-    cost_in[s] = near * weight
-
-    @pl.when(c < half)
-    def _():
-        pl.semaphore_wait(late_sem, half)
-        mirror = n_ctr - 2 - 2 * (c // 2) + c % 2
-        pl.semaphore_signal(go_sem, inc=1, device_id=(s, mirror), device_id_type=MESH)
-        late_peers(send_min)
-
     def add(r, values, sums):
         total, each = sums
         ids = wide_ids[r]
@@ -282,20 +300,14 @@
 
     def add_weight(r, sums):
         for h in range(2):
-            wide_ids[r, 4 * h : 4 * h + 4] = ids_in[h, r].astype(jnp.int32)
-        return add(r, jnp.concatenate([weight_in[0, r], weight_in[1, r]], axis=0), sums)
+            wide_ids[r, 4 * h : 4 * h + 4] = ids_in[h, r, 0].astype(jnp.int32)
+        return add(r, code_weight(jnp.concatenate([ids_in[0, r, 1], ids_in[1, r, 1]], axis=0)), sums)
 
     wait_all(ids_in.at[0], n_rows - 1, recv_sems.at[1])
-    wait_all(weight_in.at[0], n_rows - 1, recv_sems.at[2])
     partner = (s + 1 - 2 * core, c)
-    give = [
-        copy(ids_in.at[core], ids_in.at[core], 6, recv_sems.at[5], partner),
-        copy(weight_in.at[core], weight_in.at[core], 7, recv_sems.at[6], partner),
-    ]
-    for one in give:
-        one.start()
-    for one in give:
-        one.wait_recv()
+    give = copy(ids_in.at[core], ids_in.at[core], 2, recv_sems.at[2], partner)
+    give.start()
+    give.wait_recv()
     weight_sum, size = lax.fori_loop(0, n_rows, add_weight, zeros)
     weight_sum = jnp.sum(weight_sum, keepdims=True)
     size = jnp.maximum(jnp.sum(size, axis=1, keepdims=True), 1.0)
@@ -321,11 +333,11 @@
     def add_cost(d, sums):
         r, _ = row_peer(d)
         pltpu.make_async_copy(cost_in.at[r], cost_in.at[r], cost_sems.at[r]).wait()
-        return add(r, cost_in[r], sums)
-
-    cost_sum, cost = lax.fori_loop(1, n_rows, add_cost, add(s, cost_in[s], zeros))
+        return add(r, code_cost(cost_in[r]), sums)
+
+    cost_sum, own_cost = lax.fori_loop(1, n_rows, add_cost, add(s, cost, zeros))
     mean = jnp.sum(cost_sum, keepdims=True) / weight_sum
-    share = jnp.sum(cost, axis=1, keepdims=True) / (size * mean)
+    share = jnp.sum(own_cost, axis=1, keepdims=True) / (size * mean)
     diagonal = iota(own.shape, 0) == iota(own.shape, 1)
     share = jnp.sum(jnp.where(diagonal, share, 0.0), axis=0, keepdims=True)
     share_ref[...] = share[:, n_own : n_own + KO]
@@ -335,9 +347,7 @@
 
     wait_all(min_in, n_ctr - 1, send_sems.at[0])
     wait_all(ids_in.at[0], n_rows - 1, send_sems.at[1])
-    wait_all(weight_in.at[0], n_rows - 1, send_sems.at[2])
-    for one in give:
-        one.wait_send()
+    give.wait_send()
     wait_all(label_in, n_rows - 1, send_sems.at[3])
     wait_all(rows_in, n_rows - 1, send_sems.at[4])
     wait_all(cost_in, n_rows - 1, send_sems.at[5])
@@ -375,20 +385,18 @@
             pltpu.VMEM((n_rows, 16, 256), BF16),
             pltpu.VMEM((8, LANES), F32),
             pltpu.VMEM((n_ctr, 8, LANES), F32),
-            pltpu.VMEM((2, 4, LANES), IDS),
-            pltpu.VMEM((2, n_rows, 4, LANES), IDS),
+            pltpu.VMEM((2, 2, 4, LANES), CODE),
+            pltpu.VMEM((2, n_rows, 2, 4, LANES), CODE),
             pltpu.VMEM((1, LANES), F32),
             pltpu.VMEM((n_rows, 1, LANES), F32),
-            pltpu.VMEM((2, 4, LANES), F32),
-            pltpu.VMEM((2, n_rows, 4, LANES), F32),
-            pltpu.VMEM((8, LANES), F32),
-            pltpu.VMEM((n_rows, 8, LANES), F32),
+            pltpu.VMEM((8, LANES), CODE),
+            pltpu.VMEM((n_rows, 8, LANES), CODE),
             pltpu.VMEM((n_rows, 8, LANES), jnp.int32),
             pltpu.VMEM((n_rows, LANES), F32),
             pltpu.VMEM((8, LANES), F32),
             pltpu.SemaphoreType.DMA((7,)),
-            pltpu.SemaphoreType.DMA((8,)),
-            pltpu.SemaphoreType.DMA((7,)),
+            pltpu.SemaphoreType.DMA((6,)),
+            pltpu.SemaphoreType.DMA((5,)),
             pltpu.SemaphoreType.DMA((n_rows,)),
             pltpu.SemaphoreType.REGULAR,
             pltpu.SemaphoreType.REGULAR,

time: 30.7 us -> 29.7 us (0.967)
  Pallas kernels: 29.9 us -> 28.9 us
    pallas_call x1, Pallas kernels: 28.4 us -> 27.4 us  [local(): pl.pallas_call(functools.partial(kernel, n_rows, n_ctr), out_shape=(jax.S...]
where the time goes in v4:
time: 29.7 us; the launch traced here: 29.5 us
  Pallas kernels  28.9 us (97%)
  between operations  0.64 us (2%)
    pallas_call x1, Pallas kernels, local(): pl.pallas_call(functools.partial(kernel, n_rows, n_ctr), out_shape=(jax.S...  27.4 us
    pallas_call x1, Pallas kernels, local(): pl.pallas_call(deliver, out_shape=tuple((jax.ShapeDtypeStruct(x.shape, x....  1.48 us

profile of v4, /device:TPU:1, one launch (start us, length us, event | category | flops | bytes accessed | tf_op | source)
XLA Modules:
  0.0 29.5 jit_solution(2899162397327774244)
XLA Ops:
  0.6 27.4 %shard_map.67 = (f32[1,64]{1,0:T(1,128)}, f32[16,1024]{1,0:T(8,128)}, f32[1,16]{1,0:T(1,128)}) custom-call(bf16[1024,1024]{1,0:T(8,128)(2,1)} %points_hbm.1, bf16[512,1024]{1,0:T(8,128)(2,1)} %centers_hbm.1, s32[8,128]{1,0:T(8,128)} %bitcast.4, f32[8,128]{1,0:T(8,128)} %bitcast.5), custom_call_target="tpu_custom_call" | custom-call | flops 1879048192 | bytes 3145728 | tf_op jit(solution)/shard_map/pallas_call | solution.py:369
  28.0 1.5 %shard_map.68 = (f32[1,64]{1,0:T(1,128)}, f32[16,1024]{1,0:T(8,128)}, f32[1,16]{1,0:T(1,128)}) custom-call(f32[1,64]{1,0:T(1,128)} %get-tuple-element.9.refs_0_, f32[16,1024]{1,0:T(8,128)} %get-tuple-element.10.refs_1_, f32[1,16]{1,0:T(1,128)} %get-tuple-element.11.refs_2_), custom_call_target="tpu_custom_call" | custom-call | tf_op jit(solution)/shard_map/pallas_call | solution.py:414

commit v5 on v4

--- a/solution.py
+++ b/solution.py
@@ -201,49 +201,61 @@
 
     assign_load.wait()
     weight_load.wait()
-    for load in point_loads:
-        load.wait()
-    pl.when(c < half)(slots)
+    def loaded(first, last):
+        for load in point_loads[first:last]:
+            load.wait()
+
+    @pl.when(c < half)
+    def _():
+        loaded(0, 4)
+        slots()
+
+    pl.when(c >= half)(functools.partial(loaded, 0, 2))
 
     center_load.wait()
     wide = centers[...].astype(F32)
     half_norm = 0.5 * jnp.sum(wide * wide, axis=1, keepdims=True)
     for q in range(4):
+        if q == 2:
+            pl.when(c >= half)(functools.partial(loaded, 2, 4))
         some = points[q * chunk : (q + 1) * chunk, :]
-        wide = some.astype(F32)
+        least = jnp.min(half_norm - dot_nt(centers[...], some), axis=0, keepdims=True)
+        for k in range(2):
+            min_out[2 * q + k : 2 * q + k + 1, :] = least[:, k * LANES : (k + 1) * LANES]
+
+    pl.semaphore_wait(barrier, n_rows + half - 2 + c // half)
+
+    def copy(src, dst, i, recv, device):
+        return pltpu.make_async_remote_copy(
+            src, dst, send_sems.at[i], recv, device_id=device, device_id_type=MESH
+        )
+
+    def wait_all(ref, count, sem):
+        whole = ref.at[pl.ds(0, count)]
+        pltpu.make_async_copy(whole, whole, sem).wait()
+
+    def send_min(p):
+        copy(min_out, min_in.at[c], 0, recv_sems.at[0], (s, p)).start()
+
+    def tell_late(p):
+        pl.semaphore_signal(late_sem, inc=1, device_id=(s, p), device_id_type=MESH)
+
+    early_peers(send_min)
+
+    @pl.when(c >= half)
+    def _():
+        early_peers(tell_late)
+        slots()
+
+    for q in range(4):
+        wide = points[q * chunk : (q + 1) * chunk, :].astype(F32)
         wide = wide * wide
         total = wide[:, 0:LANES]
         for k in range(1, 8):
             total = total + wide[:, k * LANES : (k + 1) * LANES]
         norm = jnp.sum(total.T, axis=0, keepdims=True)
-        least = jnp.min(half_norm - dot_nt(centers[...], some), axis=0, keepdims=True)
         for k in range(2):
-            min_out[2 * q + k : 2 * q + k + 1, :] = least[:, k * LANES : (k + 1) * LANES]
             near_ref[2 * q + k : 2 * q + k + 1, :] = norm[:, k * LANES : (k + 1) * LANES]
-
-    pl.semaphore_wait(barrier, n_rows + half - 2 + c // half)
-
-    def copy(src, dst, i, recv, device):
-        return pltpu.make_async_remote_copy(
-            src, dst, send_sems.at[i], recv, device_id=device, device_id_type=MESH
-        )
-
-    def wait_all(ref, count, sem):
-        whole = ref.at[pl.ds(0, count)]
-        pltpu.make_async_copy(whole, whole, sem).wait()
-
-    def send_min(p):
-        copy(min_out, min_in.at[c], 0, recv_sems.at[0], (s, p)).start()
-
-    def tell_late(p):
-        pl.semaphore_signal(late_sem, inc=1, device_id=(s, p), device_id_type=MESH)
-
-    early_peers(send_min)
-
-    @pl.when(c >= half)
-    def _():
-        early_peers(tell_late)
-        slots()
 
     def send_half(src, dst, i):
         def send(to):
@@ -369,9 +381,9 @@
     row_share, centroid, share = pl.pallas_call(
         functools.partial(kernel, n_rows, n_ctr),
         out_shape=(
-            jax.ShapeDtypeStruct((1, slab_rows // n_ctr), F32),
-            jax.ShapeDtypeStruct((KO, width), F32),
-            jax.ShapeDtypeStruct((1, KO), F32),
+            pltpu.VMEM((1, slab_rows // n_ctr), F32),
+            pltpu.VMEM((KO, width), F32),
+            pltpu.VMEM((1, KO), F32),
         ),
         in_specs=[hbm, hbm, hbm, hbm],
         out_specs=(vmem, vmem, vmem),
@@ -402,20 +414,21 @@
             pltpu.SemaphoreType.REGULAR,
         ],
         compiler_params=pltpu.CompilerParams(
-            collective_id=0, has_side_effects=True
+            collective_id=0, has_side_effects=True, vmem_limit_bytes=48 * 1024 * 1024
         ),
         cost_estimate=pl.CostEstimate(
             flops=2 * slab_rows * width * (block + 3 * LANES),
             bytes_accessed=2 * (slab_rows + block) * width,
             transcendentals=0,
         ),
-    )(points, centers, assignment.reshape(8, LANES), row_weight.reshape(8, LANES))
+    )(*(pltpu.with_memory_space_constraint(x, pltpu.HBM) for x in (points, centers, assignment.reshape(8, LANES), row_weight.reshape(8, LANES))))
     made = (row_share, centroid, share)
     row_share, centroid, share = pl.pallas_call(
         deliver,
         out_shape=tuple(jax.ShapeDtypeStruct(x.shape, x.dtype) for x in made),
         in_specs=[vmem] * 3,
         out_specs=(vmem,) * 3,
+        compiler_params=pltpu.CompilerParams(vmem_limit_bytes=4 * 1024 * 1024),
     )(*made)
     return row_share.reshape(-1), centroid, share.reshape(-1)
 

time: 29.7 us -> 28.2 us (0.949)
  Pallas kernels: 28.9 us -> 27.4 us
    pallas_call x1, Pallas kernels: 1.48 us -> 0.64 us  [local(): pl.pallas_call(deliver, out_shape=tuple((jax.ShapeDtypeStruct(x.shape, x....]
    pallas_call x1, Pallas kernels: 27.4 us -> 26.8 us  [local(): pl.pallas_call(functools.partial(kernel, n_rows, n_ctr), out_shape=(pltpu...]
where the time goes in v5:
time: 28.2 us; the launch traced here: 28 us
  Pallas kernels  27.4 us (97%)
  between operations  0.64 us (2%)
    pallas_call x1, Pallas kernels, local(): pl.pallas_call(functools.partial(kernel, n_rows, n_ctr), out_shape=(pltpu...  26.8 us
    pallas_call x1, Pallas kernels, local(): pl.pallas_call(deliver, out_shape=tuple((jax.ShapeDtypeStruct(x.shape, x....  0.64 us

profile of v5, /device:TPU:1, one launch (start us, length us, event | category | flops | bytes accessed | tf_op | source)
XLA Modules:
  0.0 28.0 jit_solution(9331893545910129991)
XLA Ops:
  0.6 26.8 %shard_map.67 = (f32[1,64]{1,0:T(1,128)S(1)}, f32[16,1024]{1,0:T(8,128)S(1)}, f32[1,16]{1,0:T(1,128)S(1)}) custom-call(bf16[1024,1024]{1,0:T(8,128)(2,1)} %points_hbm.1, bf16[512,1024]{1,0:T(8,128)(2,1)} %centers_hbm.1, s32[8,128]{1,0:T(8,128)} %bitcast.4, f32[8,128]{1,0:T(8,128)} %bitcast.5), custom_call_target="tpu_custom_call" | custom-call | flops 1879048192 | bytes 3145728 | tf_op jit(solution)/shard_map/pallas_call | solution.py:381
  27.4 0.6 %shard_map.68 = (f32[1,64]{1,0:T(1,128)}, f32[16,1024]{1,0:T(8,128)}, f32[1,16]{1,0:T(1,128)}) custom-call(f32[1,64]{1,0:T(1,128)S(1)} %get-tuple-element.9.refs_0_, f32[16,1024]{1,0:T(8,128)S(1)} %get-tuple-element.10.refs_1_, f32[1,16]{1,0:T(1,128)S(1)} %get-tuple-element.11.refs_2_), custom_call_target="tpu_custom_call" | custom-call | tf_op jit(solution)/shard_map/pallas_call | solution.py:426

commit v6 on v5

--- a/solution.py
+++ b/solution.py
@@ -121,21 +121,14 @@
     half = n_ctr // 2
 
     def early_peers(act):
-        for d in sorted(range(half), key=lambda d: abs(2 * d - half)):
-            p = (c + d) & (half - 1)
+        for p in range(half):
             pl.when(p != c)(functools.partial(act, p))
 
     def late_peers(act):
-        for d in range(half):
-            p = half + ((c + d) & (half - 1))
+        for p in range(half, n_ctr):
             pl.when(p != c)(functools.partial(act, p))
 
     barrier = pltpu.get_barrier_semaphore()
-    assign_load = pltpu.make_async_copy(assign_hbm, assign_ref, load_sem.at[5])
-    assign_load.start()
-    weight_load = pltpu.make_async_copy(weight_hbm, weight_ref, load_sem.at[6])
-    weight_load.start()
-
     center_load = pltpu.make_async_copy(centers_hbm, centers, load_sem.at[4])
     center_load.start()
     point_loads = []
@@ -144,6 +137,10 @@
         load = pltpu.make_async_copy(points_hbm.at[part], points.at[part], load_sem.at[q])
         load.start()
         point_loads.append(load)
+    assign_load = pltpu.make_async_copy(assign_hbm, assign_ref, load_sem.at[5])
+    assign_load.start()
+    weight_load = pltpu.make_async_copy(weight_hbm, weight_ref, load_sem.at[6])
+    weight_load.start()
 
     def enter(p):
         pl.semaphore_signal(barrier, inc=1, device_id=(s, p), device_id_type=MESH)
@@ -342,12 +339,16 @@
     for q in range(4):
         centroid_ref[:, q * 256 : (q + 1) * 256] = coord[q * KO : (q + 1) * KO, :] / size[n_own:]
 
-    def add_cost(d, sums):
-        r, _ = row_peer(d)
-        pltpu.make_async_copy(cost_in.at[r], cost_in.at[r], cost_sems.at[r]).wait()
-        return add(r, code_cost(cost_in[r]), sums)
-
-    cost_sum, own_cost = lax.fori_loop(1, n_rows, add_cost, add(s, cost, zeros))
+    def add_costs(first, count, sums):
+        slabs = [row_peer(first + j)[0] for j in range(count)]
+        for r in slabs:
+            pltpu.make_async_copy(cost_in.at[r], cost_in.at[r], cost_sems.at[r]).wait()
+        for r in slabs:
+            sums = add(r, code_cost(cost_in[r]), sums)
+        return sums
+
+    sums = add_costs(1, 3, add(s, cost, zeros))
+    cost_sum, own_cost = lax.fori_loop(1, n_rows // 4, lambda k, sums: add_costs(4 * k, 4, sums), sums)
     mean = jnp.sum(cost_sum, keepdims=True) / weight_sum
     share = jnp.sum(own_cost, axis=1, keepdims=True) / (size * mean)
     diagonal = iota(own.shape, 0) == iota(own.shape, 1)

time: 28.2 us -> 27.9 us (0.989)
  Pallas kernels: 27.4 us -> 27.1 us
    pallas_call x1, Pallas kernels: 26.8 us -> 26.5 us  [local(): pl.pallas_call(functools.partial(kernel, n_rows, n_ctr), out_shape=(pltpu...]
where the time goes in v6:
time: 27.9 us; the launch traced here: 27.8 us
  Pallas kernels  27.1 us (97%)
  between operations  0.64 us (2%)
    pallas_call x1, Pallas kernels, local(): pl.pallas_call(functools.partial(kernel, n_rows, n_ctr), out_shape=(pltpu...  26.5 us
    pallas_call x1, Pallas kernels, local(): pl.pallas_call(deliver, out_shape=tuple((jax.ShapeDtypeStruct(x.shape, x....  0.64 us

profile of v6, /device:TPU:1, one launch (start us, length us, event | category | flops | bytes accessed | tf_op | source)
XLA Modules:
  0.0 27.8 jit_solution(18220078823100586174)
XLA Ops:
  0.6 26.5 %shard_map.67 = (f32[1,64]{1,0:T(1,128)S(1)}, f32[16,1024]{1,0:T(8,128)S(1)}, f32[1,16]{1,0:T(1,128)S(1)}) custom-call(bf16[1024,1024]{1,0:T(8,128)(2,1)} %points_hbm.1, bf16[512,1024]{1,0:T(8,128)(2,1)} %centers_hbm.1, s32[8,128]{1,0:T(8,128)} %bitcast.4, f32[8,128]{1,0:T(8,128)} %bitcast.5), custom_call_target="tpu_custom_call" | custom-call | flops 1879048192 | bytes 3145728 | tf_op jit(solution)/shard_map/pallas_call | solution.py:382
  27.1 0.6 %shard_map.68 = (f32[1,64]{1,0:T(1,128)}, f32[16,1024]{1,0:T(8,128)}, f32[1,16]{1,0:T(1,128)}) custom-call(f32[1,64]{1,0:T(1,128)S(1)} %get-tuple-element.9.refs_0_, f32[16,1024]{1,0:T(8,128)S(1)} %get-tuple-element.10.refs_1_, f32[1,16]{1,0:T(1,128)S(1)} %get-tuple-element.11.refs_2_), custom_call_target="tpu_custom_call" | custom-call | tf_op jit(solution)/shard_map/pallas_call | solution.py:427

commit v7 on v6

--- a/solution.py
+++ b/solution.py
@@ -244,6 +244,22 @@
         early_peers(tell_late)
         slots()
 
+    def send_half(src, dst, i):
+        def send(to):
+            h = to[0] & 1
+            copy(src.at[h], dst.at[h, s], i, recv_sems.at[i], to).start()
+
+        row_peers(send)
+
+    core = s & 1
+    send_half(ids_out, ids_in, 1)
+    row_peers(lambda to: copy(label_out, label_in.at[s], 3, recv_sems.at[3], to).start())
+    row_peers(lambda to: copy(rows_out.at[to[0]], rows_in.at[s], 4, recv_sems.at[4], to).start())
+    min_in[c] = min_out[...]
+    ids_in[core, s] = ids_out[core]
+    label_in[s] = label_out[...]
+    rows_in[s] = rows_out[s]
+
     for q in range(4):
         wide = points[q * chunk : (q + 1) * chunk, :].astype(F32)
         wide = wide * wide
@@ -253,22 +269,6 @@
         norm = jnp.sum(total.T, axis=0, keepdims=True)
         for k in range(2):
             near_ref[2 * q + k : 2 * q + k + 1, :] = norm[:, k * LANES : (k + 1) * LANES]
-
-    def send_half(src, dst, i):
-        def send(to):
-            h = to[0] & 1
-            copy(src.at[h], dst.at[h, s], i, recv_sems.at[i], to).start()
-
-        row_peers(send)
-
-    core = s & 1
-    send_half(ids_out, ids_in, 1)
-    row_peers(lambda to: copy(label_out, label_in.at[s], 3, recv_sems.at[3], to).start())
-    row_peers(lambda to: copy(rows_out.at[to[0]], rows_in.at[s], 4, recv_sems.at[4], to).start())
-    min_in[c] = min_out[...]
-    ids_in[core, s] = ids_out[core]
-    label_in[s] = label_out[...]
-    rows_in[s] = rows_out[s]
 
     @pl.when(c < half)
     def _():
@@ -368,8 +368,11 @@
 
 def deliver(*refs):
     n = len(refs) // 2
-    for i in range(n):
-        refs[n + i][...] = refs[i][...]
+    copies = [pltpu.make_async_copy(refs[i], refs[n + i], refs[-1].at[i]) for i in range(n)]
+    for copy in copies:
+        copy.start()
+    for copy in copies:
+        copy.wait()
 
 
 def local(points, centers, assignment, row_weight):
@@ -428,7 +431,8 @@
         deliver,
         out_shape=tuple(jax.ShapeDtypeStruct(x.shape, x.dtype) for x in made),
         in_specs=[vmem] * 3,
-        out_specs=(vmem,) * 3,
+        out_specs=(hbm,) * 3,
+        scratch_shapes=[pltpu.SemaphoreType.DMA((3,))],
         compiler_params=pltpu.CompilerParams(vmem_limit_bytes=4 * 1024 * 1024),
     )(*made)
     return row_share.reshape(-1), centroid, share.reshape(-1)

time: 27.9 us -> 27.9 us (level)
  no operation moved by 1% of the time
where the time goes in v7:
time: 27.9 us; the launch traced here: 27.8 us
  Pallas kernels  27.1 us (97%)
  between operations  0.64 us (2%)
    pallas_call x1, Pallas kernels, local(): pl.pallas_call(functools.partial(kernel, n_rows, n_ctr), out_shape=(pltpu...  26.5 us
    pallas_call x1, Pallas kernels, local(): pl.pallas_call(deliver, out_shape=tuple((jax.ShapeDtypeStruct(x.shape, x....  0.66 us

profile of v7, /device:TPU:1, one launch (start us, length us, event | category | flops | bytes accessed | tf_op | source)
XLA Modules:
  0.0 27.8 jit_solution(2710221400562891017)
XLA Ops:
  0.6 26.5 %shard_map.67 = (f32[1,64]{1,0:T(1,128)S(1)}, f32[16,1024]{1,0:T(8,128)S(1)}, f32[1,16]{1,0:T(1,128)S(1)}) custom-call(bf16[1024,1024]{1,0:T(8,128)(2,1)} %points_hbm.1, bf16[512,1024]{1,0:T(8,128)(2,1)} %centers_hbm.1, s32[8,128]{1,0:T(8,128)} %bitcast.4, f32[8,128]{1,0:T(8,128)} %bitcast.5), custom_call_target="tpu_custom_call" | custom-call | flops 1879048192 | bytes 3145728 | tf_op jit(solution)/shard_map/pallas_call | solution.py:385
  27.1 0.7 %shard_map.68 = (f32[1,64]{1,0:T(1,128)}, f32[16,1024]{1,0:T(8,128)}, f32[1,16]{1,0:T(1,128)}) custom-call(f32[1,64]{1,0:T(1,128)S(1)} %get-tuple-element.9.refs_0_, f32[16,1024]{1,0:T(8,128)S(1)} %get-tuple-element.10.refs_1_, f32[1,16]{1,0:T(1,128)S(1)} %get-tuple-element.11.refs_2_), custom_call_target="tpu_custom_call" | custom-call | tf_op jit(solution)/shard_map/pallas_call | solution.py:430
